TPU v7x, 128 devices: a whole 4x4x4 slice. The times are simulated.
128 devices in a mesh: section: 4 (over z), dev: 32 (over y, x, core).
Axes of the slice: x: 4, y: 4, z: 4, core: 2. Of those that a mesh axis runs over, the one named last changes fastest.
Arguments:
- points: float32 [3, 3, 524288], P(None, None, ('section', 'dev')), may hold values from -1 to 1
- weights: float32 [3, 524288], P(None, ('section', 'dev')), may hold values from 0.2 to 0.5
- density: float32 [2, 524288], P(None, ('section', 'dev')), may hold values from -6 to 6
- near_pairs: int32 [3, 16384], P(None, ('section', 'dev')), may hold values from 0 to 4095, as said below
- gap_pairs: int32 [3, 4096], P(None, ('section', 'dev')), may hold values from 0 to 4095, as said below
Outputs:
- potentials: float32 [2, 524288], P(None, ('section', 'dev'))
Inputs may be any that keep to these rules, and one draw needn't show every extreme that they name: `near_pairs`: column t belongs to device t // 128 of section+dev. Row 0 names a cluster held by that device, row 1 a cluster held by a device of the same section whose dev index differs from the owner's by at most 2, row 2 is 0 or 1. The first 32 columns of each device are the self pairs of its clusters in order and are always listed; column 32 of each device is listed and names a cluster exactly 2 dev indices away; some device lists all its columns. `gap_pairs`: column t belongs to device t // 32 of section+dev. Row 0 names a cluster held by that device, row 1 a cluster of another section held by the device of the same index along dev, row 2 is 0 or 1; some device lists all its columns.
All inputs are finite; a program needn't handle non-finite values.
Results may differ from a plain program's by a relative error of at most 0.0001.
Values sent between devices are 32-bit elements; how exact they have to be, the bound alone decides.
No kernel may reach another device: no remote copies, remote signals or barrier semaphores. Data moves between devices by JAX's collectives and lax.ppermute only.
A program may use at most 64 MiB of HBM per device.

v0:
```python
import functools
import math

import jax
import jax.numpy as jnp
from jax import lax
from jax.experimental import pallas as pl
from jax.experimental.pallas import tpu as pltpu
from jax.sharding import PartitionSpec as P

CL = 128
QUAD = 3
DEPTH = 48
TURNED = 64
UNROLL = 8
TABLE_ORDER = (4, 3, 7, 5, 6, 2, 1)

smoothing = 0.02
green_scale = 0.25 / math.pi
f32 = jnp.float32
bf16 = jnp.bfloat16


def rounded(x, magic):
    return (x + magic) - magic


def row_ids(like):
    return lax.broadcasted_iota(jnp.int32, like.shape, 0)


def parts_of(tile, row_limit):
    rows = row_ids(tile)
    live = jnp.logical_and(lax.rem(rows, 4) < 3, rows < row_limit)
    x = jnp.where(live, tile, 0.0)
    high = rounded(x, 49152.0)
    rest = x - high
    mid = rounded(rest, 96.0)
    low = rounded(rest - mid, 0.1875)
    rest = mid + low
    sq_high = high * high
    sq_rest = rest * (high + high + rest)

    def row_sum(v):
        u = v + pltpu.roll(v, 7, 0)
        return u + pltpu.roll(u, 6, 0)

    return high, mid, low, row_sum(sq_high), row_sum(sq_rest)


def square_parts(sum_high, sum_rest):
    rows = row_ids(sum_high)
    upper = rows < 4
    v = jnp.where(upper, sum_high, sum_rest)
    one = rounded(v, jnp.where(upper, 196608.0, 768.0))
    rest = v - one
    two = rounded(rest, jnp.where(upper, 768.0, 3.0))
    three = rest - two
    place = lax.rem(rows, 4)
    return jnp.where(place == 0, one, jnp.where(place == 1, two, jnp.where(place == 2, three, 0.0)))


def point_features(tile0, tile1):
    h0, m0, l0, sh0, sr0 = parts_of(tile0, 8)
    h1, m1, l1, sh1, sr1 = parts_of(tile1, 3)

    def spread(v, row):
        return jnp.broadcast_to(v[row : row + 1], v.shape)

    turn = lambda v: pltpu.roll(v, 4, 0)
    return (
        (h0, m0, l0, turn(l0), spread(sh0, 0), spread(sr0, 0)),
        (turn(h0), turn(m0), turn(l0), l0, spread(sh0, 4), spread(sr0, 4)),
        (h1, m1, l1, turn(l1), spread(sh1, 0), spread(sr1, 0)),
    )


def right_features(tile0, tile1):
    rows = row_ids(tile0)
    out = []
    for high, mid, low, low_turned, sum_high, sum_rest in point_features(tile0, tile1):
        ones = jnp.where(rows < 6, 1.0, 0.0)
        g0 = jnp.where(rows < 3, high, jnp.where(rows < 6, ones, pltpu.roll(mid, 6, 0)))
        g1 = square_parts(sum_high, sum_rest + smoothing * smoothing)
        g1 = jnp.where(rows == 7, pltpu.roll(mid, 5, 0), g1)
        g4 = jnp.where(rows < 4, mid, low_turned)
        out.append(jnp.concatenate([g0, g1, g0, g0, g4, g4], 0).astype(bf16))
    return out


def left_features(tile0, tile1):
    rows = row_ids(tile0)
    out = []
    for high, mid, low, low_turned, sum_high, sum_rest in point_features(tile0, tile1):
        sq = square_parts(sum_high, sum_rest)
        sq_high = pltpu.roll(sq, 3, 0)
        sq_rest = pltpu.roll(sq, 7, 0)
        first = rows < 3
        mids = jnp.logical_and(rows >= 3, rows < 6)
        h2 = jnp.where(first, -2.0 * high, 0.0)
        m2 = jnp.where(first, -2.0 * mid, 0.0)
        l2 = jnp.where(first, -2.0 * low, 0.0)
        b0 = jnp.where(mids, sq_high, h2)
        b1 = jnp.where(lax.rem(rows, 4) < 3, 1.0, jnp.where(rows == 7, pltpu.roll(l2, 5, 0), 0.0))
        b3 = jnp.where(rows < 6, l2, pltpu.roll(l2, 6, 0))
        b2 = jnp.where(mids, sq_rest, m2)
        b4 = h2 + pltpu.roll(h2, 4, 0)
        b5 = m2 + pltpu.roll(m2, 4, 0)
        out.append(jnp.concatenate([b0, b1, b2, b3, b4, b5], 0))
    return out


def pair_codes(here, local, others, codes):
    def lists(table, row):
        return [table[row : row + 1, k * CL : (k + 1) * CL].astype(jnp.int32) for k in range(3)]

    low5 = lambda v: jnp.bitwise_and(v, 31)
    up5 = lambda v: lax.shift_right_logical(v, 5)

    def coded(valid, here, slot, there):
        return jnp.where(valid, low5(here) + (slot * 32 + low5(there)) * 256, -1)

    first, second, listed = lists(local, 14)
    me = jnp.broadcast_to(up5(first[:, 0:1]), first.shape)
    my_dev, dev = low5(me), low5(up5(second))
    slot = jnp.full(first.shape, 4, jnp.int32)
    slot = jnp.where(dev == jnp.bitwise_xor(my_dev, 2), 3, slot)
    slot = jnp.where(dev == jnp.bitwise_xor(my_dev + 1, 1) - 1, 2, slot)
    slot = jnp.where(dev == jnp.bitwise_xor(my_dev, 1), 1, slot)
    slot = jnp.where(dev == my_dev, 0, slot)
    inside = slot == 0
    if here:
        codes[0:1, :] = coded(jnp.logical_and(listed > 0, inside), first, 0, second)
        inside = jnp.logical_and(inside, first != second)
        codes[1:2, :] = coded(jnp.logical_and(listed > 0, inside), second, 0, first)
        return
    codes[0:1, :] = coded(jnp.logical_and(listed > 0, slot > 0), first, slot, second)
    for slot_in in range(1, 5):
        first, second, listed = lists(others[slot_in - 1], 14)
        valid = jnp.logical_and(listed > 0, up5(second) == me)
        codes[slot_in : slot_in + 1, :] = coded(valid, second, slot_in, first)
    first, second, listed = lists(local, 15)
    slot = 4 + jnp.bitwise_xor(up5(me), up5(up5(second)))
    row = coded(listed > 0, first, slot, second)
    lanes = lax.broadcasted_iota(jnp.int32, row.shape, 1)
    for slot_in in range(5, 8):
        first, second, listed = lists(others[slot_in - 1], 15)
        valid = jnp.logical_and(listed > 0, up5(second) == me)
        incoming = coded(valid, second, slot_in, first)
        row = jnp.where(lanes < 32 * (slot_in - 4), row, pltpu.roll(incoming, 32 * (slot_in - 4), 1))
    codes[5:6, :] = row


WIDE = 8


def pair_kernel(here, clusters, *refs):
    tables = refs[:1] if here else refs[:8]
    local = tables[0]
    refs = refs[len(tables) :]
    if not here:
        tables = [local] + [tables[1 + TABLE_ORDER.index(slot)] for slot in range(1, 8)]
    if here:
        left, wide_w, acc = refs[:3]
        refs = refs[3:]
    else:
        left, wide_w, _, out, acc = refs[:5]
        refs = refs[5:]
    codes, codes_smem, sem, todo, right, raw = refs
    used = tables if here else tables[1:]
    base = 0 if here else clusters

    pair_codes(here, local, tables[1:], codes)
    lists_copy = pltpu.make_async_copy(codes, codes_smem, sem)
    lists_copy.start()

    def prepare_left(n, carry):
        for u in range(WIDE):
            c = n * WIDE + u
            lanes = pl.ds(pl.multiple_of(c * CL, CL), CL)
            tile0, tile1 = local[0:8, lanes], local[8:16, lanes]
            weight_rows = (tile0[3:4], tile0[7:8], tile1[3:4])
            for q, block in enumerate(left_features(tile0, tile1)):
                weight = jnp.broadcast_to(weight_rows[q] * green_scale, (8, CL))
                block = jnp.concatenate([block, weight, jnp.zeros((TURNED - DEPTH - 8, CL), f32)], 0)
                turned = jnp.transpose(block)
                left[c, q * CL : (q + 1) * CL, 0:TURNED] = turned.astype(bf16)
                wide_w[c, q * CL : (q + 1) * CL, :] = jnp.broadcast_to(turned[:, DEPTH : DEPTH + 1], (CL, CL))
            acc[c] = jnp.zeros((CL, CL), f32)
        return carry

    if here:
        lax.fori_loop(0, clusters // WIDE, prepare_left, 0)
    lists_copy.wait()

    steps = clusters // WIDE
    rows_of_codes = 2 if here else 6
    count = 0
    for table in range(len(used)):

        def prepare_right(n, count):
            lanes = pl.ds(pl.multiple_of(n * (WIDE * CL), WIDE * CL), WIDE * CL)
            tile0, tile1 = used[table][0:8, lanes], used[table][8:16, lanes]
            blocks = right_features(tile0, tile1)
            for u in range(WIDE):
                place = table * clusters + n * WIDE + u
                cut = slice(u * CL, (u + 1) * CL)
                for q in range(QUAD):
                    right[place, :, q * CL : (q + 1) * CL] = blocks[q][:, cut]
                raw[place, 0:8, :] = tile0[:, cut]
                raw[place, 8:16, :] = tile1[:, cut]
            rows = range(2) if here else ([table] if table < 6 else [])
            for row in rows:
                for u in range(CL // steps):
                    code = codes_smem[row, n * (CL // steps) + u]
                    todo[count] = code
                    count = count + (code >= 0).astype(jnp.int32)
            return count

        count = lax.fori_loop(0, steps, prepare_right, count)
    for extra in range(UNROLL - 1):
        todo[count + extra] = clusters + base * 256

    def tile_of(i, j):
        weight_b = (raw[j, 3:4, :], raw[j, 7:8, :], raw[j, 11:12, :])
        far = right[j]
        total = None
        for p in range(QUAD):
            near = left[i, p * CL : (p + 1) * CL, 0:DEPTH]
            dist = jnp.dot(near, far, preferred_element_type=f32)
            row = None
            for q in range(QUAD):
                term = weight_b[q] * lax.rsqrt(dist[:, q * CL : (q + 1) * CL])
                row = term if row is None else row + term
            row = row * wide_w[i, p * CL : (p + 1) * CL, :]
            total = row if total is None else total + row
        return total

    lower = lax.broadcasted_iota(jnp.int32, (1, CL), 1) < CL // 2

    def group(g, carry):
        done = []
        for u in range(UNROLL):
            code = todo[g * UNROLL + u]
            i = jnp.bitwise_and(code, 255)
            j = lax.shift_right_logical(code, 8) - base
            done.append((i, j, tile_of(i, j)))
        for i, j, tile in done:
            dens0, dens1 = raw[j, 12:13, :], raw[j, 13:14, :]
            same = tile * jnp.where(lower, dens0, dens1)
            other = tile * jnp.where(lower, dens1, dens0)
            acc[i] += same + pltpu.roll(other, CL // 2, 1)
        return carry

    lax.fori_loop(0, lax.div(count + UNROLL - 1, UNROLL), group, 0)

    if here:
        return

    rows = lax.broadcasted_iota(jnp.int32, (8, 2 * CL), 0)
    lanes_of = jnp.bitwise_and(lax.broadcasted_iota(jnp.int32, (8, 2 * CL), 1), CL - 1)
    chosen = jnp.where(rows == lanes_of // (CL // 2), 1.0, 0.0).astype(bf16)

    def finish(n, carry):
        for u in range(8):
            c = n * 8 + u
            lanes = pl.ds(pl.multiple_of(c * CL, CL), CL)
            value = acc[c]
            high = value.astype(bf16)
            low = (value - high.astype(f32)).astype(bf16)
            both = jnp.concatenate([high, low], 1)
            sums = lax.dot_general(chosen, both, (((1,), (1,)), ((), ())), preferred_element_type=f32)
            out[:, lanes] = sums[0:2]
        return carry

    lax.fori_loop(0, clusters // 8, finish, 0)


def pair_sums(tables, kept=None):
    here = kept is None
    panels = tables[0].shape[1]
    clusters = panels // CL
    places = (1 if here else len(tables) - 1) * clusters
    whole = pl.BlockSpec(memory_space=pltpu.VMEM)
    result = jax.ShapeDtypeStruct((2, panels), f32)
    left = jax.ShapeDtypeStruct((clusters + 1, QUAD * CL, CL), bf16)
    wide = jax.ShapeDtypeStruct((clusters + 1, QUAD * CL, CL), f32)
    acc = jax.ShapeDtypeStruct((clusters + 1, CL, CL), f32)
    return pl.pallas_call(
        functools.partial(pair_kernel, here, clusters),
        out_shape=[left, wide, acc] if here else [result, acc],
        in_specs=[whole] * (len(tables) + (0 if here else 3)),
        out_specs=[whole] * (3 if here else 2),
        input_output_aliases={} if here else {len(tables) + 2: 1},
        scratch_shapes=[
            pltpu.VMEM((8, CL), jnp.int32),
            pltpu.SMEM((8, CL), jnp.int32),
            pltpu.SemaphoreType.DMA,
            pltpu.SMEM((8 * CL + UNROLL,), jnp.int32),
            pltpu.VMEM((places, DEPTH, QUAD * CL), bf16),
            pltpu.VMEM((places, 16, CL), f32),
        ],
        compiler_params=pltpu.CompilerParams(vmem_limit_bytes=32 * 1024 * 1024),
        cost_estimate=pl.CostEstimate(
            flops=2_000_000_000, bytes_accessed=(40 if here else 80) * 1024 * 1024, transcendentals=10_000_000
        ),
        name="pairs_here" if here else "pairs_across",
    )(*tables, *(kept or ()))


def pack_kernel(*refs):
    sent, out = refs[5:7]
    points, weights, density, near_pairs, gap_pairs = refs[7:12]
    copies = [pltpu.make_async_copy(refs[k], refs[7 + k], refs[12].at[k]) for k in range(5)]
    for copy in copies:
        copy.start()
    for copy in copies:
        copy.wait()
    for q in range(QUAD):
        for c in range(3):
            out[4 * q + c : 4 * q + c + 1, :] = points[c, q : q + 1, :]
        out[4 * q + 3 : 4 * q + 4, :] = weights[q : q + 1, :]
    out[12:14, :] = density[...]
    out[14:16, :] = jnp.zeros((2, out.shape[1]), f32)
    for k in range(3):
        out[14:15, k * CL : k * CL + near_pairs.shape[1]] = near_pairs[k : k + 1, :].astype(f32)
        out[15:16, k * CL : k * CL + gap_pairs.shape[1]] = gap_pairs[k : k + 1, :].astype(f32)
    sent[...] = out[...]


def packed(points, weights, density, near_pairs, gap_pairs):
    whole = pl.BlockSpec(memory_space=pltpu.VMEM)
    return pl.pallas_call(
        pack_kernel,
        out_shape=[jax.ShapeDtypeStruct((16, points.shape[2]), f32)] * 2,
        in_specs=[pl.BlockSpec(memory_space=pltpu.HBM)] * 5,
        out_specs=[whole] * 2,
        scratch_shapes=[pltpu.VMEM(x.shape, x.dtype) for x in (points, weights, density, near_pairs, gap_pairs)]
        + [pltpu.SemaphoreType.DMA((5,))],
        compiler_params=pltpu.CompilerParams(vmem_limit_bytes=8 * 1024 * 1024),
        name="pack",
    )(*[pltpu.with_memory_space_constraint(x, pltpu.HBM) for x in (points, weights, density, near_pairs, gap_pairs)])


near_partners = (
    lambda i: i ^ 1,
    lambda i: ((i + 1) ^ 1) - 1,
    lambda i: i ^ 2,
    lambda i: ((i + 2) ^ 2) - 2,
)


def swapped(block, axis, partner):
    size = lax.axis_size(axis)
    route = [(i, partner(i)) for i in range(size) if 0 <= partner(i) < size]
    return lax.ppermute(block, axis, route)


def per_device(points, weights, density, near_pairs, gap_pairs):
    sent, local = packed(points, weights, density, near_pairs, gap_pairs)
    tables = [local]
    for slot in TABLE_ORDER:
        if slot > 4:
            tables.append(swapped(sent, "section", lambda i, k=slot - 4: i ^ k))
        else:
            tables.append(swapped(sent, "dev", near_partners[slot - 1]))
    kept = pair_sums(tables[:1])
    return pair_sums(tables, kept)[0]


def solution(mesh):
    placed = (
        P(None, None, ("section", "dev")),
        P(None, ("section", "dev")),
        P(None, ("section", "dev")),
        P(None, ("section", "dev")),
        P(None, ("section", "dev")),
    )
    return jax.shard_map(
        per_device,
        mesh=mesh,
        in_specs=placed,
        out_specs=P(None, ("section", "dev")),
        check_vma=False,
    )
```

profile of v0, /device:TPU:41, one launch (start us, length us, event | category | flops | bytes accessed | tf_op | source)
XLA Modules:
  0.0 53.4 jit_solution(6219257092250819257)
XLA Ops:
  0.0 1.1 %pack.1 = (f32[16,4096]{1,0:T(8,128)S(1)}, f32[16,4096]{1,0:T(8,128)S(1)}) custom-call(f32[3,3,4096]{2,1,0:T(4,128)} %refs_0_.1, f32[3,4096]{1,0:T(4,128)} %refs_1_.1, f32[2,4096]{1,0:T(2,128)} %refs_2_.1, s32[3,128]{1,0:T(4,128)} %refs_3_.1, s32[3,32]{1,0:T(4,128)} %refs_4_.1), custom_call_target="tpu_custom_call" | custom-call | tf_op jit(solution)/shard_map/pack/pallas_call | solution.py:333
  1.1 0.8 %collective-permute-start.6 = (f32[16,4096]{1,0:T(8,128)S(1)}, f32[16,4096]{1,0:T(8,128)S(1)}, u32[]{:S(2)}, u32[]{:S(2)}) collective-permute-start(f32[16,4096]{1,0:T(8,128)S(1)} %get-tuple-element.12), channel_id=1, source_target_pairs={{0,1},{1,0},{2,3},{3,2},{4,5},{5,4},{6,7},{7,6},{8,9},{9,8},{10,11... | collective-permute-start | bytes 786440 | tf_op jit(solution)/shard_map/ppermute | solution.py:356
  1.8 3.0 %collective-permute-start.5 = (f32[16,4096]{1,0:T(8,128)S(1)}, f32[16,4096]{1,0:T(8,128)S(1)}, u32[]{:S(2)}, u32[]{:S(2)}) collective-permute-start(f32[16,4096]{1,0:T(8,128)S(1)} %get-tuple-element.12), channel_id=1, source_target_pairs={{1,2},{2,1},{3,4},{4,3},{5,6},{6,5},{7,8},{8,7},{9,10},{10,9},{11,... | collective-permute-start | bytes 786440 | tf_op jit(solution)/shard_map/ppermute | solution.py:356
  4.8 2.8 %collective-permute-start.4 = (f32[16,4096]{1,0:T(8,128)S(1)}, f32[16,4096]{1,0:T(8,128)S(1)}, u32[]{:S(2)}, u32[]{:S(2)}) collective-permute-start(f32[16,4096]{1,0:T(8,128)S(1)} %get-tuple-element.12), channel_id=1, source_target_pairs={{0,64},{32,96},{64,0},{96,32},{1,65},{33,97},{65,1},{97,33},{2,66}... | collective-permute-start | bytes 786440 | tf_op jit(solution)/shard_map/ppermute | solution.py:356
  7.6 0.7 %collective-permute-start.3 = (f32[16,4096]{1,0:T(8,128)S(1)}, f32[16,4096]{1,0:T(8,128)S(1)}, u32[]{:S(2)}, u32[]{:S(2)}) collective-permute-start(f32[16,4096]{1,0:T(8,128)S(1)} %get-tuple-element.12), channel_id=1, source_target_pairs={{0,32},{32,0},{64,96},{96,64},{1,33},{33,1},{65,97},{97,65},{2,34}... | collective-permute-start | bytes 786440 | tf_op jit(solution)/shard_map/ppermute | solution.py:356
  8.4 0.0 collective-permute-start.2
  8.4 0.0 collective-permute-done.6.refs_7_
  8.4 1.2 %collective-permute-start.1 = (f32[16,4096]{1,0:T(8,128)S(1)}, f32[16,4096]{1,0:T(8,128)S(1)}, u32[]{:S(2)}, u32[]{:S(2)}) collective-permute-start(f32[16,4096]{1,0:T(8,128)S(1)} %get-tuple-element.12), channel_id=1, source_target_pairs={{0,2},{1,3},{2,0},{3,1},{4,6},{5,7},{6,4},{7,5},{8,10},{9,11},{10,... | collective-permute-start | bytes 786440 | tf_op jit(solution)/shard_map/ppermute | solution.py:356
  9.6 0.2 collective-permute-done.5.refs_6_
  9.8 6.1 %collective-permute-start = (f32[16,4096]{1,0:T(8,128)S(1)}, f32[16,4096]{1,0:T(8,128)S(1)}, u32[]{:S(2)}, u32[]{:S(2)}) collective-permute-start(f32[16,4096]{1,0:T(8,128)S(1)} %get-tuple-element.12), channel_id=1, source_target_pairs={{2,4},{3,5},{4,2},{5,3},{6,8},{7,9},{8,6},{9,7},{10,12},{11,13},{1... | collective-permute-start | bytes 786440 | tf_op jit(solution)/shard_map/ppermute | solution.py:356
  15.9 12.7 %pairs_here.1 = (bf16[33,384,128]{2,1,0:T(8,128)(2,1)S(1)}, f32[33,384,128]{2,1,0:T(8,128)S(1)}, f32[33,128,128]{2,1,0:T(8,128)S(1)}) custom-call(f32[16,4096]{1,0:T(8,128)S(1)} %get-tuple-element.11.refs_0_), custom_call_target="tpu_custom_call" | custom-call | flops 2000000000 | bytes 41943040 | tf_op jit(solution)/shard_map/pairs_here/pallas_call | solution.py:289
  28.6 0.0 collective-permute-done.4.refs_5_
  28.6 0.0 collective-permute-done.3.refs_4_
  28.6 0.0 collective-permute-done.2.refs_3_
  28.6 0.0 collective-permute-done.1.refs_2_
  28.6 0.0 collective-permute-done.refs_1_
  28.6 24.8 %pairs_across.1 = (f32[2,4096]{1,0:T(2,128)}, f32[33,128,128]{2,1,0:T(8,128)S(1)}) custom-call(f32[16,4096]{1,0:T(8,128)S(1)} %get-tuple-element.11.refs_0_, f32[16,4096]{1,0:T(8,128)S(1)} %collective-permute-done.refs_1_, f32[16,4096]{1,0:T(8,128)S(1)} %collective-permute-done.1.refs_2_, ...), custom_call_target="tpu_custom_call", output_to_operand_aliasing={{1}: (10, {})} | custom-call | flops 2000000000 | bytes 83886080 | tf_op jit(solution)/shard_map/pairs_across/pallas_call | solution.py:289
Async XLA Ops:
  1.1 7.3 %collective-permute-start.6 = (f32[16,4096]{1,0:T(8,128)S(1)}, f32[16,4096]{1,0:T(8,128)S(1)}, u32[]{:S(2)}, u32[]{:S(2)}) collective-permute-start(f32[16,4096]{1,0:T(8,128)S(1)} %get-tuple-element.12), channel_id=1, source_target_pairs={{0,1},{1,0},{2,3},{3,2},{4,5},{5,4},{6,7},{7,6},{8,9},{9,8},{10,11... | collective-permute-start | bytes 786440 | tf_op jit(solution)/shard_map/ppermute | solution.py:356
  1.8 8.0 %collective-permute-start.5 = (f32[16,4096]{1,0:T(8,128)S(1)}, f32[16,4096]{1,0:T(8,128)S(1)}, u32[]{:S(2)}, u32[]{:S(2)}) collective-permute-start(f32[16,4096]{1,0:T(8,128)S(1)} %get-tuple-element.12), channel_id=1, source_target_pairs={{1,2},{2,1},{3,4},{4,3},{5,6},{6,5},{7,8},{8,7},{9,10},{10,9},{11,... | collective-permute-start | bytes 786440 | tf_op jit(solution)/shard_map/ppermute | solution.py:356
  4.8 23.7 %collective-permute-start.4 = (f32[16,4096]{1,0:T(8,128)S(1)}, f32[16,4096]{1,0:T(8,128)S(1)}, u32[]{:S(2)}, u32[]{:S(2)}) collective-permute-start(f32[16,4096]{1,0:T(8,128)S(1)} %get-tuple-element.12), channel_id=1, source_target_pairs={{0,64},{32,96},{64,0},{96,32},{1,65},{33,97},{65,1},{97,33},{2,66}... | collective-permute-start | bytes 786440 | tf_op jit(solution)/shard_map/ppermute | solution.py:356
  7.6 21.0 %collective-permute-start.3 = (f32[16,4096]{1,0:T(8,128)S(1)}, f32[16,4096]{1,0:T(8,128)S(1)}, u32[]{:S(2)}, u32[]{:S(2)}) collective-permute-start(f32[16,4096]{1,0:T(8,128)S(1)} %get-tuple-element.12), channel_id=1, source_target_pairs={{0,32},{32,0},{64,96},{96,64},{1,33},{33,1},{65,97},{97,65},{2,34}... | collective-permute-start | bytes 786440 | tf_op jit(solution)/shard_map/ppermute | solution.py:356
  8.4 20.3 %collective-permute-start.2 = (f32[16,4096]{1,0:T(8,128)S(1)}, f32[16,4096]{1,0:T(8,128)S(1)}, u32[]{:S(2)}, u32[]{:S(2)}) collective-permute-start(f32[16,4096]{1,0:T(8,128)S(1)} %get-tuple-element.12), channel_id=1, source_target_pairs={{0,96},{32,64},{64,32},{96,0},{1,97},{33,65},{65,33},{97,1},{2,98}... | collective-permute-start | bytes 786440 | tf_op jit(solution)/shard_map/ppermute | solution.py:356
  8.4 20.3 %collective-permute-start.1 = (f32[16,4096]{1,0:T(8,128)S(1)}, f32[16,4096]{1,0:T(8,128)S(1)}, u32[]{:S(2)}, u32[]{:S(2)}) collective-permute-start(f32[16,4096]{1,0:T(8,128)S(1)} %get-tuple-element.12), channel_id=1, source_target_pairs={{0,2},{1,3},{2,0},{3,1},{4,6},{5,7},{6,4},{7,5},{8,10},{9,11},{10,... | collective-permute-start | bytes 786440 | tf_op jit(solution)/shard_map/ppermute | solution.py:356
  9.8 18.8 %collective-permute-start = (f32[16,4096]{1,0:T(8,128)S(1)}, f32[16,4096]{1,0:T(8,128)S(1)}, u32[]{:S(2)}, u32[]{:S(2)}) collective-permute-start(f32[16,4096]{1,0:T(8,128)S(1)} %get-tuple-element.12), channel_id=1, source_target_pairs={{2,4},{3,5},{4,2},{5,3},{6,8},{7,9},{8,6},{9,7},{10,12},{11,13},{1... | collective-permute-start | bytes 786440 | tf_op jit(solution)/shard_map/ppermute | solution.py:356
where the time goes:
time: 53.7 us; the launch traced here: 53.4 us
  Pallas kernels  38.5 us (72%)
  starting transfers between devices  14.6 us (27%)
    pallas_call x2, Pallas kernels, pair_sums(): pl.pallas_call(functools.partial(pair_kernel, here, clusters), out_shape=...  37.5 us
    ppermute x7, starting transfers between devices, swapped(): return lax.ppermute(block, axis, route)  14.6 us
  transfers between devices with their start and end apart: 7, of which 1 were waited for; matrix products, arithmetic and copies ran while one was open for 0% of the time, Pallas kernels for 24%

commit v1 on v0

--- a/solution.py
+++ b/solution.py
@@ -12,7 +12,7 @@
 QUAD = 3
 DEPTH = 48
 TURNED = 64
-UNROLL = 8
+UNROLL = 12
 TABLE_ORDER = (4, 3, 7, 5, 6, 2, 1)
 
 smoothing = 0.02

time: 53.7 us -> 53.9 us (level)
  the two profiles are of different devices: /device:TPU:41 before, /device:TPU:121 now
where the time goes in v1:
time: 53.9 us; the launch traced here: 53.2 us
  Pallas kernels  37.7 us (70%)
  starting transfers between devices  15 us (28%)
    pallas_call x2, Pallas kernels, pair_sums(): pl.pallas_call(functools.partial(pair_kernel, here, clusters), out_shape=...  36.7 us
    ppermute x7, starting transfers between devices, swapped(): return lax.ppermute(block, axis, route)  15 us
  transfers between devices with their start and end apart: 7, of which 1 were waited for; matrix products, arithmetic and copies ran while one was open for 0% of the time, Pallas kernels for 20%

profile of v1, /device:TPU:121, one launch (start us, length us, event | category | flops | bytes accessed | tf_op | source)
XLA Modules:
  0.0 53.2 jit_solution(9554282173747373929)
XLA Ops:
  0.0 1.1 %pack.1 = (f32[16,4096]{1,0:T(8,128)S(1)}, f32[16,4096]{1,0:T(8,128)S(1)}) custom-call(f32[3,3,4096]{2,1,0:T(4,128)} %refs_0_.1, f32[3,4096]{1,0:T(4,128)} %refs_1_.1, f32[2,4096]{1,0:T(2,128)} %refs_2_.1, s32[3,128]{1,0:T(4,128)} %refs_3_.1, s32[3,32]{1,0:T(4,128)} %refs_4_.1), custom_call_target="tpu_custom_call" | custom-call | tf_op jit(solution)/shard_map/pack/pallas_call | solution.py:333
  1.1 0.8 %collective-permute-start.6 = (f32[16,4096]{1,0:T(8,128)S(1)}, f32[16,4096]{1,0:T(8,128)S(1)}, u32[]{:S(2)}, u32[]{:S(2)}) collective-permute-start(f32[16,4096]{1,0:T(8,128)S(1)} %get-tuple-element.12), channel_id=1, source_target_pairs={{0,1},{1,0},{2,3},{3,2},{4,5},{5,4},{6,7},{7,6},{8,9},{9,8},{10,11... | collective-permute-start | bytes 786440 | tf_op jit(solution)/shard_map/ppermute | solution.py:356
  1.8 3.0 %collective-permute-start.5 = (f32[16,4096]{1,0:T(8,128)S(1)}, f32[16,4096]{1,0:T(8,128)S(1)}, u32[]{:S(2)}, u32[]{:S(2)}) collective-permute-start(f32[16,4096]{1,0:T(8,128)S(1)} %get-tuple-element.12), channel_id=1, source_target_pairs={{1,2},{2,1},{3,4},{4,3},{5,6},{6,5},{7,8},{8,7},{9,10},{10,9},{11,... | collective-permute-start | bytes 786440 | tf_op jit(solution)/shard_map/ppermute | solution.py:356
  4.8 0.4 collective-permute-start.4
  5.2 0.0 collective-permute-start.3
  5.2 3.0 %collective-permute-start.2 = (f32[16,4096]{1,0:T(8,128)S(1)}, f32[16,4096]{1,0:T(8,128)S(1)}, u32[]{:S(2)}, u32[]{:S(2)}) collective-permute-start(f32[16,4096]{1,0:T(8,128)S(1)} %get-tuple-element.12), channel_id=1, source_target_pairs={{0,96},{32,64},{64,32},{96,0},{1,97},{33,65},{65,33},{97,1},{2,98}... | collective-permute-start | bytes 786440 | tf_op jit(solution)/shard_map/ppermute | solution.py:356
  8.2 0.0 collective-permute-done.6.refs_7_
  8.2 1.2 %collective-permute-start.1 = (f32[16,4096]{1,0:T(8,128)S(1)}, f32[16,4096]{1,0:T(8,128)S(1)}, u32[]{:S(2)}, u32[]{:S(2)}) collective-permute-start(f32[16,4096]{1,0:T(8,128)S(1)} %get-tuple-element.12), channel_id=1, source_target_pairs={{0,2},{1,3},{2,0},{3,1},{4,6},{5,7},{6,4},{7,5},{8,10},{9,11},{10,... | collective-permute-start | bytes 786440 | tf_op jit(solution)/shard_map/ppermute | solution.py:356
  9.4 0.4 collective-permute-done.5.refs_6_
  9.8 6.7 %collective-permute-start = (f32[16,4096]{1,0:T(8,128)S(1)}, f32[16,4096]{1,0:T(8,128)S(1)}, u32[]{:S(2)}, u32[]{:S(2)}) collective-permute-start(f32[16,4096]{1,0:T(8,128)S(1)} %get-tuple-element.12), channel_id=1, source_target_pairs={{2,4},{3,5},{4,2},{5,3},{6,8},{7,9},{8,6},{9,7},{10,12},{11,13},{1... | collective-permute-start | bytes 786440 | tf_op jit(solution)/shard_map/ppermute | solution.py:356
  16.5 10.9 %pairs_here.1 = (bf16[33,384,128]{2,1,0:T(8,128)(2,1)S(1)}, f32[33,384,128]{2,1,0:T(8,128)S(1)}, f32[33,128,128]{2,1,0:T(8,128)S(1)}) custom-call(f32[16,4096]{1,0:T(8,128)S(1)} %get-tuple-element.11.refs_0_), custom_call_target="tpu_custom_call" | custom-call | flops 2000000000 | bytes 41943040 | tf_op jit(solution)/shard_map/pairs_here/pallas_call | solution.py:289
  27.4 0.0 collective-permute-done.4.refs_5_
  27.4 0.0 collective-permute-done.3.refs_4_
  27.4 0.0 collective-permute-done.2.refs_3_
  27.4 0.0 collective-permute-done.1.refs_2_
  27.4 0.0 collective-permute-done.refs_1_
  27.4 25.8 %pairs_across.1 = (f32[2,4096]{1,0:T(2,128)}, f32[33,128,128]{2,1,0:T(8,128)S(1)}) custom-call(f32[16,4096]{1,0:T(8,128)S(1)} %get-tuple-element.11.refs_0_, f32[16,4096]{1,0:T(8,128)S(1)} %collective-permute-done.refs_1_, f32[16,4096]{1,0:T(8,128)S(1)} %collective-permute-done.1.refs_2_, ...), custom_call_target="tpu_custom_call", output_to_operand_aliasing={{1}: (10, {})} | custom-call | flops 2000000000 | bytes 83886080 | tf_op jit(solution)/shard_map/pairs_across/pallas_call | solution.py:289
Async XLA Ops:
  1.1 7.1 %collective-permute-start.6 = (f32[16,4096]{1,0:T(8,128)S(1)}, f32[16,4096]{1,0:T(8,128)S(1)}, u32[]{:S(2)}, u32[]{:S(2)}) collective-permute-start(f32[16,4096]{1,0:T(8,128)S(1)} %get-tuple-element.12), channel_id=1, source_target_pairs={{0,1},{1,0},{2,3},{3,2},{4,5},{5,4},{6,7},{7,6},{8,9},{9,8},{10,11... | collective-permute-start | bytes 786440 | tf_op jit(solution)/shard_map/ppermute | solution.py:356
  1.8 8.0 %collective-permute-start.5 = (f32[16,4096]{1,0:T(8,128)S(1)}, f32[16,4096]{1,0:T(8,128)S(1)}, u32[]{:S(2)}, u32[]{:S(2)}) collective-permute-start(f32[16,4096]{1,0:T(8,128)S(1)} %get-tuple-element.12), channel_id=1, source_target_pairs={{1,2},{2,1},{3,4},{4,3},{5,6},{6,5},{7,8},{8,7},{9,10},{10,9},{11,... | collective-permute-start | bytes 786440 | tf_op jit(solution)/shard_map/ppermute | solution.py:356
  4.8 22.5 %collective-permute-start.4 = (f32[16,4096]{1,0:T(8,128)S(1)}, f32[16,4096]{1,0:T(8,128)S(1)}, u32[]{:S(2)}, u32[]{:S(2)}) collective-permute-start(f32[16,4096]{1,0:T(8,128)S(1)} %get-tuple-element.12), channel_id=1, source_target_pairs={{0,64},{32,96},{64,0},{96,32},{1,65},{33,97},{65,1},{97,33},{2,66}... | collective-permute-start | bytes 786440 | tf_op jit(solution)/shard_map/ppermute | solution.py:356
  5.2 22.2 %collective-permute-start.3 = (f32[16,4096]{1,0:T(8,128)S(1)}, f32[16,4096]{1,0:T(8,128)S(1)}, u32[]{:S(2)}, u32[]{:S(2)}) collective-permute-start(f32[16,4096]{1,0:T(8,128)S(1)} %get-tuple-element.12), channel_id=1, source_target_pairs={{0,32},{32,0},{64,96},{96,64},{1,33},{33,1},{65,97},{97,65},{2,34}... | collective-permute-start | bytes 786440 | tf_op jit(solution)/shard_map/ppermute | solution.py:356
  5.2 22.2 %collective-permute-start.2 = (f32[16,4096]{1,0:T(8,128)S(1)}, f32[16,4096]{1,0:T(8,128)S(1)}, u32[]{:S(2)}, u32[]{:S(2)}) collective-permute-start(f32[16,4096]{1,0:T(8,128)S(1)} %get-tuple-element.12), channel_id=1, source_target_pairs={{0,96},{32,64},{64,32},{96,0},{1,97},{33,65},{65,33},{97,1},{2,98}... | collective-permute-start | bytes 786440 | tf_op jit(solution)/shard_map/ppermute | solution.py:356
  8.2 19.2 %collective-permute-start.1 = (f32[16,4096]{1,0:T(8,128)S(1)}, f32[16,4096]{1,0:T(8,128)S(1)}, u32[]{:S(2)}, u32[]{:S(2)}) collective-permute-start(f32[16,4096]{1,0:T(8,128)S(1)} %get-tuple-element.12), channel_id=1, source_target_pairs={{0,2},{1,3},{2,0},{3,1},{4,6},{5,7},{6,4},{7,5},{8,10},{9,11},{10,... | collective-permute-start | bytes 786440 | tf_op jit(solution)/shard_map/ppermute | solution.py:356
  9.8 17.6 %collective-permute-start = (f32[16,4096]{1,0:T(8,128)S(1)}, f32[16,4096]{1,0:T(8,128)S(1)}, u32[]{:S(2)}, u32[]{:S(2)}) collective-permute-start(f32[16,4096]{1,0:T(8,128)S(1)} %get-tuple-element.12), channel_id=1, source_target_pairs={{2,4},{3,5},{4,2},{5,3},{6,8},{7,9},{8,6},{9,7},{10,12},{11,13},{1... | collective-permute-start | bytes 786440 | tf_op jit(solution)/shard_map/ppermute | solution.py:356

commit v2 on v1

--- a/solution.py
+++ b/solution.py
@@ -13,7 +13,7 @@
 DEPTH = 48
 TURNED = 64
 UNROLL = 12
-TABLE_ORDER = (4, 3, 7, 5, 6, 2, 1)
+TABLE_ORDER = (3, 7, 4, 5, 6, 2, 1)
 
 smoothing = 0.02
 green_scale = 0.25 / math.pi

time: 53.9 us -> 51.7 us (0.959)
  the two profiles are of different devices: /device:TPU:121 before, /device:TPU:93 now
where the time goes in v2:
time: 51.7 us; the launch traced here: 50.8 us
  Pallas kernels  41.3 us (80%)
  starting transfers between devices  9.35 us (18%)
    pallas_call x2, Pallas kernels, pair_sums(): pl.pallas_call(functools.partial(pair_kernel, here, clusters), out_shape=...  40.3 us
    ppermute x7, starting transfers between devices, swapped(): return lax.ppermute(block, axis, route)  9.35 us
    pallas_call x1, Pallas kernels, packed(): pl.pallas_call(pack_kernel, out_shape=[jax.ShapeDtypeStruct((16, points.s...  1.06 us
  transfers between devices with their start and end apart: 7, of which 0 were waited for; matrix products, arithmetic and copies ran while one was open for 0% of the time, Pallas kernels for 26%

profile of v2, /device:TPU:93, one launch (start us, length us, event | category | flops | bytes accessed | tf_op | source)
XLA Modules:
  0.0 50.8 jit_solution(701780438209165562)
XLA Ops:
  0.0 1.1 %pack.1 = (f32[16,4096]{1,0:T(8,128)S(1)}, f32[16,4096]{1,0:T(8,128)S(1)}) custom-call(f32[3,3,4096]{2,1,0:T(4,128)} %refs_0_.1, f32[3,4096]{1,0:T(4,128)} %refs_1_.1, f32[2,4096]{1,0:T(2,128)} %refs_2_.1, s32[3,128]{1,0:T(4,128)} %refs_3_.1, s32[3,32]{1,0:T(4,128)} %refs_4_.1), custom_call_target="tpu_custom_call" | custom-call | tf_op jit(solution)/shard_map/pack/pallas_call | solution.py:333
  1.1 0.8 %collective-permute-start.6 = (f32[16,4096]{1,0:T(8,128)S(1)}, f32[16,4096]{1,0:T(8,128)S(1)}, u32[]{:S(2)}, u32[]{:S(2)}) collective-permute-start(f32[16,4096]{1,0:T(8,128)S(1)} %get-tuple-element.12), channel_id=1, source_target_pairs={{0,1},{1,0},{2,3},{3,2},{4,5},{5,4},{6,7},{7,6},{8,9},{9,8},{10,11... | collective-permute-start | bytes 786440 | tf_op jit(solution)/shard_map/ppermute | solution.py:356
  1.8 2.7 %collective-permute-start.5 = (f32[16,4096]{1,0:T(8,128)S(1)}, f32[16,4096]{1,0:T(8,128)S(1)}, u32[]{:S(2)}, u32[]{:S(2)}) collective-permute-start(f32[16,4096]{1,0:T(8,128)S(1)} %get-tuple-element.12), channel_id=1, source_target_pairs={{1,2},{2,1},{3,4},{4,3},{5,6},{6,5},{7,8},{8,7},{9,10},{10,9},{11,... | collective-permute-start | bytes 786440 | tf_op jit(solution)/shard_map/ppermute | solution.py:356
  4.6 0.1 collective-permute-start.4
  4.6 1.6 %collective-permute-start.3 = (f32[16,4096]{1,0:T(8,128)S(1)}, f32[16,4096]{1,0:T(8,128)S(1)}, u32[]{:S(2)}, u32[]{:S(2)}) collective-permute-start(f32[16,4096]{1,0:T(8,128)S(1)} %get-tuple-element.12), channel_id=1, source_target_pairs={{0,32},{32,0},{64,96},{96,64},{1,33},{33,1},{65,97},{97,65},{2,34}... | collective-permute-start | bytes 786440 | tf_op jit(solution)/shard_map/ppermute | solution.py:356
  6.3 2.4 %collective-permute-start.2 = (f32[16,4096]{1,0:T(8,128)S(1)}, f32[16,4096]{1,0:T(8,128)S(1)}, u32[]{:S(2)}, u32[]{:S(2)}) collective-permute-start(f32[16,4096]{1,0:T(8,128)S(1)} %get-tuple-element.12), channel_id=1, source_target_pairs={{2,4},{3,5},{4,2},{5,3},{6,8},{7,9},{8,6},{9,7},{10,12},{11,13},{1... | collective-permute-start | bytes 786440 | tf_op jit(solution)/shard_map/ppermute | solution.py:356
  8.7 0.0 collective-permute-done.6.refs_7_
  8.7 1.7 %collective-permute-start.1 = (f32[16,4096]{1,0:T(8,128)S(1)}, f32[16,4096]{1,0:T(8,128)S(1)}, u32[]{:S(2)}, u32[]{:S(2)}) collective-permute-start(f32[16,4096]{1,0:T(8,128)S(1)} %get-tuple-element.12), channel_id=1, source_target_pairs={{0,96},{32,64},{64,32},{96,0},{1,97},{33,65},{65,33},{97,1},{2,98}... | collective-permute-start | bytes 786440 | tf_op jit(solution)/shard_map/ppermute | solution.py:356
  10.4 0.0 collective-permute-done.5.refs_6_
  10.4 0.0 collective-permute-start
  10.4 13.3 %pairs_here.1 = (bf16[33,384,128]{2,1,0:T(8,128)(2,1)S(1)}, f32[33,384,128]{2,1,0:T(8,128)S(1)}, f32[33,128,128]{2,1,0:T(8,128)S(1)}) custom-call(f32[16,4096]{1,0:T(8,128)S(1)} %get-tuple-element.11.refs_0_), custom_call_target="tpu_custom_call" | custom-call | flops 2000000000 | bytes 41943040 | tf_op jit(solution)/shard_map/pairs_here/pallas_call | solution.py:289
  23.8 0.0 collective-permute-done.4.refs_5_
  23.8 0.0 collective-permute-done.3.refs_4_
  23.8 0.0 collective-permute-done.2.refs_3_
  23.8 0.0 collective-permute-done.1.refs_2_
  23.8 0.0 collective-permute-done.refs_1_
  23.8 27.0 %pairs_across.1 = (f32[2,4096]{1,0:T(2,128)}, f32[33,128,128]{2,1,0:T(8,128)S(1)}) custom-call(f32[16,4096]{1,0:T(8,128)S(1)} %get-tuple-element.11.refs_0_, f32[16,4096]{1,0:T(8,128)S(1)} %collective-permute-done.refs_1_, f32[16,4096]{1,0:T(8,128)S(1)} %collective-permute-done.1.refs_2_, ...), custom_call_target="tpu_custom_call", output_to_operand_aliasing={{1}: (10, {})} | custom-call | flops 2000000000 | bytes 83886080 | tf_op jit(solution)/shard_map/pairs_across/pallas_call | solution.py:289
Async XLA Ops:
  1.1 7.7 %collective-permute-start.6 = (f32[16,4096]{1,0:T(8,128)S(1)}, f32[16,4096]{1,0:T(8,128)S(1)}, u32[]{:S(2)}, u32[]{:S(2)}) collective-permute-start(f32[16,4096]{1,0:T(8,128)S(1)} %get-tuple-element.12), channel_id=1, source_target_pairs={{0,1},{1,0},{2,3},{3,2},{4,5},{5,4},{6,7},{7,6},{8,9},{9,8},{10,11... | collective-permute-start | bytes 786440 | tf_op jit(solution)/shard_map/ppermute | solution.py:356
  1.8 8.6 %collective-permute-start.5 = (f32[16,4096]{1,0:T(8,128)S(1)}, f32[16,4096]{1,0:T(8,128)S(1)}, u32[]{:S(2)}, u32[]{:S(2)}) collective-permute-start(f32[16,4096]{1,0:T(8,128)S(1)} %get-tuple-element.12), channel_id=1, source_target_pairs={{1,2},{2,1},{3,4},{4,3},{5,6},{6,5},{7,8},{8,7},{9,10},{10,9},{11,... | collective-permute-start | bytes 786440 | tf_op jit(solution)/shard_map/ppermute | solution.py:356
  4.6 19.2 %collective-permute-start.4 = (f32[16,4096]{1,0:T(8,128)S(1)}, f32[16,4096]{1,0:T(8,128)S(1)}, u32[]{:S(2)}, u32[]{:S(2)}) collective-permute-start(f32[16,4096]{1,0:T(8,128)S(1)} %get-tuple-element.12), channel_id=1, source_target_pairs={{0,64},{32,96},{64,0},{96,32},{1,65},{33,97},{65,1},{97,33},{2,66}... | collective-permute-start | bytes 786440 | tf_op jit(solution)/shard_map/ppermute | solution.py:356
  4.6 19.1 %collective-permute-start.3 = (f32[16,4096]{1,0:T(8,128)S(1)}, f32[16,4096]{1,0:T(8,128)S(1)}, u32[]{:S(2)}, u32[]{:S(2)}) collective-permute-start(f32[16,4096]{1,0:T(8,128)S(1)} %get-tuple-element.12), channel_id=1, source_target_pairs={{0,32},{32,0},{64,96},{96,64},{1,33},{33,1},{65,97},{97,65},{2,34}... | collective-permute-start | bytes 786440 | tf_op jit(solution)/shard_map/ppermute | solution.py:356
  6.3 17.5 %collective-permute-start.2 = (f32[16,4096]{1,0:T(8,128)S(1)}, f32[16,4096]{1,0:T(8,128)S(1)}, u32[]{:S(2)}, u32[]{:S(2)}) collective-permute-start(f32[16,4096]{1,0:T(8,128)S(1)} %get-tuple-element.12), channel_id=1, source_target_pairs={{2,4},{3,5},{4,2},{5,3},{6,8},{7,9},{8,6},{9,7},{10,12},{11,13},{1... | collective-permute-start | bytes 786440 | tf_op jit(solution)/shard_map/ppermute | solution.py:356
  8.7 15.1 %collective-permute-start.1 = (f32[16,4096]{1,0:T(8,128)S(1)}, f32[16,4096]{1,0:T(8,128)S(1)}, u32[]{:S(2)}, u32[]{:S(2)}) collective-permute-start(f32[16,4096]{1,0:T(8,128)S(1)} %get-tuple-element.12), channel_id=1, source_target_pairs={{0,96},{32,64},{64,32},{96,0},{1,97},{33,65},{65,33},{97,1},{2,98}... | collective-permute-start | bytes 786440 | tf_op jit(solution)/shard_map/ppermute | solution.py:356
  10.4 13.4 %collective-permute-start = (f32[16,4096]{1,0:T(8,128)S(1)}, f32[16,4096]{1,0:T(8,128)S(1)}, u32[]{:S(2)}, u32[]{:S(2)}) collective-permute-start(f32[16,4096]{1,0:T(8,128)S(1)} %get-tuple-element.12), channel_id=1, source_target_pairs={{0,2},{1,3},{2,0},{3,1},{4,6},{5,7},{6,4},{7,5},{8,10},{9,11},{10,... | collective-permute-start | bytes 786440 | tf_op jit(solution)/shard_map/ppermute | solution.py:356
